TPU v7x, 32 devices: a whole 2x2x4 slice. The times are simulated.
32 devices in a mesh: groups: 2 (over x), seq: 16 (over z, y, core).
Axes of the slice: x: 2, y: 2, z: 4, core: 2. Of those that a mesh axis runs over, the one named last changes fastest.
Arguments:
- tokens: bfloat16 [4096, 1536], P(('groups', 'seq')), parts along dimension 0, may hold values from -6 to 6
- control: bfloat16 [4096, 1536], P(('groups', 'seq')), parts along dimension 0, may hold values from -1800 to 1800, as said below
- zero_weight: bfloat16 [1536, 1536], P(None, 'seq'), may hold values from -0.15625 to 0.15625
- modulation: float32 [6, 1536], P('groups'), parts along dimension 0, may hold values from -1 to 1.5, as said below
- qkv_weight: bfloat16 [1536, 2304], replicated, may hold values from -0.15625 to 0.15625
- out_weight: bfloat16 [768, 1536], replicated, may hold values from -0.21875 to 0.21875
Outputs:
- block_out: bfloat16 [4096, 1536], P(('groups', 'seq')), parts along dimension 0
There are 2 independent parts, one for each index of `groups`. A program takes and returns all parts, laid end to end along the dimension named above; an argument that names none is the same for every part. Nothing has to cross between parts.
Inputs may be any that keep to these rules, and one draw needn't show every extreme that they name: Features of the control block, of varied scales. `modulation`: row 0 shifts, row 1 scales, row 2 gates.
All inputs are finite; a program needn't handle non-finite values.
Results may differ from a plain program's by a relative error of at most 0.025.
Values may be sent and summed in bfloat16 or wider, within the bound.
A program may use at most 192 MiB of HBM per device.

v0:
```python
import math

import jax
import jax.numpy as jnp
from jax import lax
from jax.sharding import PartitionSpec as P

HEADS = 12
HEAD = 64
GROUPS = 32
VIEWS = 8


def make_absorb(query_heads):
    query_rows = query_heads.shape[0]
    head_count = query_heads.shape[1]
    head_size = query_heads.shape[2]
    scale = 1.0 / math.sqrt(head_size)

    def absorb(carry, piece, start):
        best, total, accum = carry
        key_piece, value_piece = piece
        length = key_piece.shape[0]
        scores = (
            jnp.einsum(
                "qhd,khd->hqk",
                query_heads,
                key_piece.reshape(length, head_count, head_size),
                preferred_element_type=jnp.float32,
            )
            * scale
        )
        new_best = jnp.maximum(best, jnp.max(scores, axis=-1))
        shrink = jnp.exp(best - new_best)
        expo = jnp.exp(scores - new_best[:, :, None])
        total = jnp.sum(expo, axis=-1)
        mixed = jnp.einsum(
            "hqk,khd->qhd",
            expo.astype(jnp.bfloat16),
            value_piece.reshape(length, head_count, head_size),
            preferred_element_type=jnp.float32,
        )
        accum = accum * jnp.repeat(jnp.transpose(shrink), head_size, axis=1) + mixed.reshape(
            query_rows, head_count * head_size
        )
        return (new_best, total, accum)

    start_carry = (
        jnp.full((head_count, query_rows), -1e30, jnp.float32),
        jnp.zeros((head_count, query_rows), jnp.float32),
        jnp.zeros((query_rows, head_count * head_size), jnp.float32),
    )
    return (absorb, start_carry)


def finish(result, head_size):
    best, total, accum = result
    return (accum / jnp.repeat(jnp.transpose(total), head_size, axis=1)).astype(jnp.bfloat16)


def per_device(tokens, control, zero_weight, modulation, qkv_weight, out_weight):
    rows = tokens.shape[0]
    width = tokens.shape[1]
    per_group = width // GROUPS
    devices = lax.axis_size("seq")
    span = devices // VIEWS
    my_view = lax.axis_index("seq") // span
    picker = (jnp.arange(VIEWS) == my_view).astype(jnp.float32)[:, None]
    count = float(rows * span * per_group)
    control_f = control.astype(jnp.float32).reshape(rows, GROUPS, per_group)
    local_sums = jnp.sum(control_f, axis=(0, 2))
    mean_table = lax.psum(picker * local_sums[None, :], "seq")
    view_mean = jnp.sum(picker * mean_table, axis=0) / count
    centered = control_f - view_mean[None, :, None]
    local_squares = jnp.sum(centered * centered, axis=(0, 2))
    spread_table = lax.psum(picker * local_squares[None, :], "seq")
    view_var = jnp.sum(picker * spread_table, axis=0) / count
    normed = (
        (centered / jnp.sqrt(view_var + 1e-05)[None, :, None])
        .reshape(rows, width)
        .astype(jnp.bfloat16)
    )
    residual = jnp.dot(
        normed,
        lax.all_gather(zero_weight, "seq", axis=1, tiled=True),
        preferred_element_type=jnp.float32,
    )
    hidden_f = (tokens.astype(jnp.float32) + residual).astype(jnp.bfloat16).astype(jnp.float32)
    tok_mean = jnp.mean(hidden_f, axis=-1, keepdims=True)
    tok_dev = hidden_f - tok_mean
    tok_var = jnp.mean(tok_dev * tok_dev, axis=-1, keepdims=True)
    layered = tok_dev / jnp.sqrt(tok_var + 1e-06)
    adapted = (layered * (1.0 + modulation[1]) + modulation[0]).astype(jnp.bfloat16)
    projected = jnp.dot(adapted, qkv_weight, preferred_element_type=jnp.float32)
    features = HEADS * HEAD
    query_local = projected[:, :features].astype(jnp.bfloat16)
    key_local = projected[:, features : 2 * features].astype(jnp.bfloat16)
    value_local = projected[:, 2 * features :].astype(jnp.bfloat16)
    absorb, start_carry = make_absorb(query_local.reshape(rows, HEADS, HEAD))
    result = absorb(
        start_carry,
        (
            lax.all_gather(key_local, "seq", axis=0, tiled=True),
            lax.all_gather(value_local, "seq", axis=0, tiled=True),
        ),
        jnp.int32(0),
    )
    attended = finish(result, HEAD)
    projected_out = jnp.dot(attended, out_weight, preferred_element_type=jnp.float32)
    return (hidden_f + modulation[2] * projected_out).astype(jnp.bfloat16)


def solution(mesh):
    placed = (
        P(("groups", "seq"), None),
        P(("groups", "seq"), None),
        P(None, "seq"),
        P("groups", None),
        P(),
        P(),
    )
    return jax.shard_map(
        per_device,
        mesh=mesh,
        in_specs=placed,
        out_specs=P(("groups", "seq"), None),
        check_vma=False,
    )
```

profile of v0, /device:TPU:0, one launch (start us, length us, event | category | flops | bytes accessed | tf_op | source)
XLA Modules:
  0.0 192.8 jit_solution(11947615145444555500)
XLA Ops:
  6.5 0.0 copy-start
  6.5 0.0 all-gather.4.cloned.1.call-start
  6.5 0.7 all-gather.4.cloned.1.call-update
  7.3 0.0 all-gather.6.cloned.1.call-start
  7.3 1.1 convert_reduce_fusion
  8.4 0.1 reduce_sum.78
  8.5 0.1 reduce_sum.79
  8.6 0.1 broadcast_multiply_fusion.1
  8.7 35.2 %psum.14 = f32[8,32]{1,0:T(8,128)S(1)} all-reduce(f32[8,32]{1,0:T(8,128)S(1)} %broadcast_multiply_fusion.1), channel_id=1, replica_groups=mesh['groups'=2,'seq'=16] {'seq'}, use_global_device_ids=true, to_apply=%region_2.3 | all-reduce | flops 256 | bytes 2048 | tf_op jit(solution)/shard_map/psum | solution.py:72
  43.9 0.1 multiply_reduce_fusion.3
  43.9 0.1 sub.40
  44.0 0.1 sub.41
  44.1 1.1 fusion.24
  45.2 0.1 reduce_sum.82
  45.3 0.1 reduce_sum.83
  45.4 0.1 broadcast_multiply_fusion
  45.5 29.8 %psum.15 = f32[8,32]{1,0:T(8,128)S(1)} all-reduce(f32[8,32]{1,0:T(8,128)S(1)} %broadcast_multiply_fusion), channel_id=1, replica_groups=mesh['groups'=2,'seq'=16] {'seq'}, use_global_device_ids=true, to_apply=%region_6.7 | all-reduce | flops 256 | bytes 2048 | tf_op jit(solution)/shard_map/psum | solution.py:76
  75.3 0.1 multiply_reduce_fusion.2
  75.4 0.1 div.50
  75.5 0.1 div.51
  75.5 0.9 slice_reduce_fusion.1
  76.4 0.0 all-gather.4.cloned.1.call-done
  76.5 0.0 copy-start.2
  76.5 4.4 %fusion.35 = (f32[128]{0:T(128)S(1)}, f32[128,1536]{1,0:T(8,128)S(1)}) fusion(bf16[1536,1536]{0,1:T(8,128)(2,1)} %all-gather.4.cloned.1.call-done, bf16[128,1536]{1,0:T(8,128)(2,1)} %param.7, f32[1536]{0:T(1024)S(1)} %div.51, f32[1536]{0:T(1024)S(1)} %sub.41, bf16[128,1536]{1,0:T(8,128)(2,1)} %param.6), kind=kOutput, calls=%fused_computation.48 | convolution fusion | flops 605749120 | bytes 6304256 | tf_op jit(solution)/shard_map/dot_general | solution.py:83
  80.9 0.2 multiply_reduce_fusion.1
  81.2 0.0 copy-done.2
  81.2 1.2 convolution_convert_fusion
  82.4 0.8 fusion.34
  83.2 0.0 all-gather.6.cloned.1.call-update
  83.2 0.0 all-gather.8.cloned.1.call-start
  83.2 0.7 all-gather.8.cloned.1.call-update
  83.9 0.2 copy.13
  84.1 41.6 %all-gather.6.cloned.1.call-done = bf16[2048,768]{1,0:T(8,128)(2,1)} async-done(((bf16[128,768]{1,0:T(8,128)(2,1)}), bf16[2048,768]{1,0:T(8,128)(2,1)}) %all-gather.6.cloned.1.call-update) | async-done | bytes 3145744 | tf_op jit(solution)/shard_map/all_gather | solution.py:103
  125.7 4.7 %copy.14 = bf16[2048,768]{0,1:T(8,128)(2,1)} copy(bf16[2048,768]{1,0:T(8,128)(2,1)} %all-gather.6.cloned.1.call-done) | data formatting | bytes 6291456 | tf_op jit(solution)/shard_map/all_gather | solution.py:103
  130.4 3.8 %multiply_reduce_fusion = (f32[12,128]{1,0:T(8,128)S(1)}, f32[12,128,2048]{2,1,0:T(8,128)S(1)}) fusion(bf16[128,12,64]{0,2,1:T(8,128)(2,1)S(1)} %bitcast.25, bf16[2048,12,64]{0,2,1:T(8,128)(2,1)} %bitcast.22), kind=kOutput, calls=%fused_computation.1 | convolution fusion | flops 408943104 | bytes 15931392 | tf_op jit(solution)/shard_map/qhd,khd->hqk/dot_general | solution.py:25
  134.2 0.0 copy-start.1
  134.2 4.5 %copy-done.1 = f32[12,128,2048]{2,1,0:T(8,128)} copy-done((f32[12,128,2048]{2,1,0:T(8,128)}, f32[12,128,2048]{2,1,0:T(8,128)S(1)}, u32[]{:S(2)}) %copy-start.1) | copy-done | bytes 12582936
  138.8 2.4 %fusion = f32[12,128]{1,0:T(8,128)S(1)} fusion(f32[12,128,2048]{2,1,0:T(8,128)S(1)} %get-tuple-element.16, f32[12,128]{1,0:T(8,128)S(1)} %get-tuple-element.12), kind=kLoop, calls=%fused_computation.2 | loop fusion | flops 9435648 | bytes 12595200 | tf_op jit(solution)/shard_map/reduce_sum | solution.py:36
  141.2 30.8 %all-gather.8.cloned.1.call-done = bf16[2048,768]{1,0:T(8,128)(2,1)} async-done(((bf16[128,768]{1,0:T(8,128)(2,1)}), bf16[2048,768]{1,0:T(8,128)(2,1)}) %all-gather.8.cloned.1.call-update) | async-done | bytes 3145744 | tf_op jit(solution)/shard_map/all_gather | solution.py:104
  172.0 4.7 %copy.15 = bf16[2048,768]{0,1:T(8,128)(2,1)} copy(bf16[2048,768]{1,0:T(8,128)(2,1)} %all-gather.8.cloned.1.call-done) | data formatting | bytes 6291456 | tf_op jit(solution)/shard_map/all_gather | solution.py:104
  176.7 8.3 %fusion.19 = bf16[128,12,64]{0,2,1:T(8,128)(2,1)S(1)} fusion(bf16[2048,12,64]{0,2,1:T(8,128)(2,1)} %bitcast.23, f32[12,128,2048]{2,1,0:T(8,128)} %copy-done.1, f32[12,128]{1,0:T(8,128)S(1)} %get-tuple-element.12, f32[128,12]{0,1:T(8,128)S(1)} %bitcast.26, f32[128,12]{0,1:T(8,128)S(1)} %get-tuple-element.11), kind=kOutput, calls=%fused_computation.17 | convolution fusion | flops 412385280 | bytes 15943680 | tf_op jit(solution)/shard_map/hqk,khd->qhd/dot_general | solution.py:37
  185.0 0.0 copy-done
  185.0 1.3 fusion.7
  (6 shorter events, 0.0 us)
Async XLA Ops:
  6.5 178.5 %copy-start = (bf16[768,1536]{1,0:T(8,128)(2,1)S(1)}, bf16[768,1536]{1,0:T(8,128)(2,1)}, u32[]{:S(2)}) copy-start(bf16[768,1536]{1,0:T(8,128)(2,1)} %param.11) | copy-start | bytes 7077892
  6.5 69.9 %all-gather.4.cloned.1.call-start = ((), (), s32[]{:S(2)}) async-start(), calls=%async_computation | async-start | bytes 5013504 | tf_op jit(solution)/shard_map/all_gather | solution.py:85
  7.3 118.4 %all-gather.6.cloned.1.call-start = ((), (), s32[]{:S(2)}) async-start(), calls=%async_computation.1 | async-start | bytes 3342336 | tf_op jit(solution)/shard_map/all_gather | solution.py:103
  76.5 4.7 %copy-start.2 = (bf16[1536,2304]{1,0:T(8,128)(2,1)S(1)}, bf16[1536,2304]{1,0:T(8,128)(2,1)}, u32[]{:S(2)}) copy-start(bf16[1536,2304]{1,0:T(8,128)(2,1)} %param.10) | copy-start | bytes 21233668
  83.2 88.8 %all-gather.8.cloned.1.call-start = ((), (), s32[]{:S(2)}) async-start(), calls=%async_computation.2 | async-start | bytes 3342336 | tf_op jit(solution)/shard_map/all_gather | solution.py:104
  134.2 4.6 %copy-start.1 = (f32[12,128,2048]{2,1,0:T(8,128)}, f32[12,128,2048]{2,1,0:T(8,128)S(1)}, u32[]{:S(2)}) copy-start(f32[12,128,2048]{2,1,0:T(8,128)S(1)} %get-tuple-element.16) | copy-start | bytes 37748740
Sparse Core Ops, SparseCore 0:
  9.6 56.6 all-gather.3
  83.3 42.3 all-gather.5
  128.0 43.9 all-gather.7
where the time goes:
time: 193 us
  waiting for transfers between devices  73.8 us (38%)
  blocking collectives  65 us (34%)
  matrix products  19 us (10%)
  local copies, waits for them, and re-layouts  15.4 us (8%)
  between operations  13.2 us (7%)
  other arithmetic  6.37 us (3%)
    all_gather x1, waiting for transfers between devices, per_device(): lax.all_gather(key_local, 'seq', axis=0, tiled=True)  41.6 us
    psum x1, blocking collectives, per_device(): mean_table = lax.psum(picker * local_sums[None, :], 'seq')  35.2 us
    all_gather x1, waiting for transfers between devices, per_device(): lax.all_gather(value_local, 'seq', axis=0, tiled=True)  30.8 us
    psum x1, blocking collectives, per_device(): spread_table = lax.psum(picker * local_squares[None, :], 'seq')  29.8 us
    dot_general x1, matrix products, absorb(): jnp.einsum('hqk,khd->qhd', expo.astype(jnp.bfloat16), value_piece.reshape...  8.27 us
    all_gather x1, local copies, waits for them, and re-layouts, per_device(): lax.all_gather(value_local, 'seq', axis=0, tiled=True)  4.71 us
    all_gather x1, local copies, waits for them, and re-layouts, per_device(): lax.all_gather(key_local, 'seq', axis=0, tiled=True)  4.71 us
    unnamed x6, local copies, waits for them, and re-layouts  4.56 us
  transfers between devices with their start and end apart: 3, of which 2 were waited for; matrix products, arithmetic and copies ran while one was open for 8% of the time, Pallas kernels for 0%

commit v1 on v0

v1 whole, which is shorter than its diff:
```python
import functools

import jax
import jax.numpy as jnp
from jax import lax
from jax.experimental import pallas as pl
from jax.experimental.pallas import tpu as pltpu
from jax.sharding import PartitionSpec as P

HEADS = 12
HEAD = 64
GROUPS = 32
VIEWS = 8
SPLIT = 4
LANES = 128
MESH = pl.DeviceIdType.MESH


def flip(index, d):
    if d == 0:
        return index
    if d == 1:
        return index + 1 - 2 * (index % 2)
    if d == 2:
        return index + 2 - 4 * (index // 2)
    return 3 - index


def kernel(
    n,
    gather,
    tokens_ref,
    control_ref,
    w_ref,
    mod_ref,
    qkv_hbm,
    out_hbm,
    result_ref,
    wbuf,
    qkv_w,
    out_w,
    stat,
    hidden,
    adapted,
    pack,
    qpack,
    kvb,
    qbuf,
    obuf,
    osend,
    m_ref,
    l_ref,
    acc_ref,
    load_sem,
    stat_s,
    stat_r,
    wz_s,
    wz_r,
    wy_s,
    wy_r,
    wx_s,
    wx_r,
    wc_s,
    wc_r,
    kz_s,
    kz_r,
    ky_s,
    ky_r,
    kc_s,
    kc_r,
    q_s,
    q_r,
    o_s,
    o_r,
):
    rows, width = tokens_ref.shape
    per_group = width // GROUPS
    cols = width // n
    members = n // SPLIT
    pairs = members // 2
    span = n // VIEWS
    me_g = lax.axis_index("groups")
    me = lax.axis_index("seq")
    hh = me // members
    uu = (me % members) // 2
    cc = me % 2

    def at(h, u, c):
        return (me_g, (h * pairs + u) * 2 + c)

    sibling = at(hh, uu, 1 - cc)
    zmate = [at(flip(hh, d), uu, cc) for d in range(SPLIT)]
    ymate = [at(hh, (uu + f) % pairs, cc) for f in range(pairs)]
    xmate = (1 - me_g, me)
    view_base = (me // span) * span
    peer = [(me_g, view_base + (me - view_base + f) % span) for f in range(span)]

    loads = [
        pltpu.make_async_copy(qkv_hbm, qkv_w, load_sem.at[0]),
        pltpu.make_async_copy(out_hbm, out_w, load_sem.at[1]),
    ]
    if not gather:
        loads.append(pltpu.make_async_copy(w_ref, wbuf, load_sem.at[2]))
    for load in loads:
        load.start()

    barrier = pltpu.get_barrier_semaphore()
    greet = [sibling] + zmate[1:] + ymate[1:] + peer[1:] + ([xmate] if gather else [])
    for device in greet:
        pl.semaphore_signal(barrier, inc=1, device_id=device, device_id_type=MESH)

    if gather:
        wbuf[pl.ds(pl.multiple_of(me * cols, cols), cols), :] = jnp.transpose(w_ref[...])

    pl.semaphore_wait(barrier, len(greet))

    sent = []

    def send(src, dst, ssem, rsem, device):
        copy = pltpu.make_async_remote_copy(
            src_ref=src, dst_ref=dst, send_sem=ssem, recv_sem=rsem, device_id=device, device_id_type=MESH
        )
        copy.start()
        sent.append(copy)

    def arrive(dst, ssem, rsem):
        pltpu.make_async_remote_copy(
            src_ref=dst, dst_ref=dst, send_sem=ssem, recv_sem=rsem, device_id=sibling, device_id_type=MESH
        ).wait_recv()

    third = cols // 3

    def slab(e, d, c, start, count):
        owner = (flip(hh, d) * pairs + (uu + e) % pairs) * 2 + c
        return wbuf.at[pl.ds(pl.multiple_of(owner * cols + start, third), count), :]

    plane = third * me_g
    over_x = 2 * third * me_g
    from_x = 2 * third * (1 - me_g)

    def relay_y(d):
        for f in range(1, pairs):
            part = slab(0, d, cc, plane, 2 * third)
            send(part, part, wy_s.at[f, d], wy_r.at[f, d], ymate[f])

    def relay_x(e, d):
        part = slab(e, d, cc, over_x, third)
        send(part, part, wx_s.at[e, d], wx_r.at[e, d], xmate)

    def relay_c(e, d):
        part = slab(e, d, cc, plane, 2 * third)
        send(part, part, wc_s.at[0, e, d], wc_r.at[0, e, d], sibling)

    if gather:
        own = slab(0, 0, cc, plane, 2 * third)
        for d in range(1, SPLIT):
            send(own, own, wz_s.at[d], wz_r.at[d], zmate[d])
        relay_y(0)
        whole = slab(0, 0, cc, 0, cols)
        send(whole, whole, wc_s.at[0, 0, 0], wc_r.at[0, 0, 0], sibling)

    lane_group = lax.broadcasted_iota(jnp.int32, (width, LANES), 1) * per_group
    channel = lax.broadcasted_iota(jnp.int32, (width, LANES), 0)
    member = ((channel >= lane_group) & (channel < lane_group + per_group)).astype(jnp.float32)

    def group_sum(line):
        return lax.dot_general(
            line,
            member,
            (((1,), (0,)), ((), ())),
            precision=lax.Precision.HIGHEST,
            preferred_element_type=jnp.float32,
        )

    def spread(line):
        return lax.dot_general(
            line,
            member,
            (((1,), (1,)), ((), ())),
            precision=lax.Precision.HIGHEST,
            preferred_element_type=jnp.float32,
        )

    local_count = float(rows * per_group)
    control_f = control_ref[...].astype(jnp.float32)
    col_sum = jnp.sum(control_f, axis=0, keepdims=True)
    local_mean = group_sum(jnp.broadcast_to(col_sum, (8, width))) / local_count
    off = control_f - spread(local_mean)[0:1, :]
    col_sq = jnp.sum(off * off, axis=0, keepdims=True)
    local_m2 = group_sum(jnp.broadcast_to(col_sq, (8, width)))
    stat[0, 0] = local_mean
    stat[0, 1] = local_m2
    for f in range(1, span):
        send(stat.at[0], stat.at[f], stat_s.at[f], stat_r.at[f], peer[f])
    for f in range(1, span):
        arrive(stat.at[f], stat_s.at[f], stat_r.at[f])
    mean = stat[0, 0]
    m2 = stat[0, 1]
    for f in range(1, span):
        mean = mean + stat[f, 0]
        m2 = m2 + stat[f, 1]
    mean = mean / span
    for f in range(span):
        gap = stat[f, 0] - mean
        m2 = m2 + local_count * (gap * gap)
    var = m2 / (local_count * span)
    inv = 1.0 / jnp.sqrt(var + 1e-05)
    normed = ((control_ref[...].astype(jnp.float32) - spread(mean)[0:1, :]) * spread(inv)[0:1, :]).astype(
        jnp.bfloat16
    )

    if gather:
        for d in range(1, SPLIT):
            arrive(slab(0, d, cc, plane, 2 * third), wz_s.at[d], wz_r.at[d])
            relay_y(d)
            relay_x(0, d)
            relay_c(0, d)
            for e in range(1, pairs):
                f = pairs - e
                arrive(slab(e, d - 1, cc, plane, 2 * third), wy_s.at[f, d - 1], wy_r.at[f, d - 1])
                relay_x(e, d - 1)
                relay_c(e, d - 1)
        for e in range(1, pairs):
            f = pairs - e
            d = SPLIT - 1
            arrive(slab(e, d, cc, plane, 2 * third), wy_s.at[f, d], wy_r.at[f, d])
            relay_x(e, d)
            relay_c(e, d)
        order = [(0, d) for d in range(1, SPLIT)] + [(e, d) for d in range(SPLIT) for e in range(1, pairs)]
        for e, d in order:
            part = slab(e, d, cc, from_x, third)
            arrive(part, wx_s.at[e, d], wx_r.at[e, d])
            send(part, part, wc_s.at[1, e, d], wc_r.at[1, e, d], sibling)
    else:
        loads[2].wait()

    block = width // SPLIT
    for d in range(SPLIT):
        if gather:
            for e in range(pairs):
                if (e, d) == (0, 0):
                    arrive(slab(0, 0, 1 - cc, 0, cols), wc_s.at[0, 0, 0], wc_r.at[0, 0, 0])
                else:
                    arrive(slab(e, d, 1 - cc, plane, 2 * third), wc_s.at[0, e, d], wc_r.at[0, e, d])
                    arrive(slab(e, d, 1 - cc, from_x, third), wc_s.at[1, e, d], wc_r.at[1, e, d])
        place = pl.ds(pl.multiple_of(flip(hh, d) * block, block), block)
        residual = lax.dot_general(
            normed, wbuf[place, :], (((1,), (1,)), ((), ())), preferred_element_type=jnp.float32
        )
        hidden[:, place] = (tokens_ref[:, place].astype(jnp.float32) + residual).astype(jnp.bfloat16)

    hidden_f = hidden[...].astype(jnp.float32)
    tok_mean = jnp.mean(hidden_f, axis=-1, keepdims=True)
    tok_dev = hidden_f - tok_mean
    tok_var = jnp.mean(tok_dev * tok_dev, axis=-1, keepdims=True)
    layered = tok_dev / jnp.sqrt(tok_var + 1e-06)
    adapted[...] = (layered * (1.0 + mod_ref[1:2, :]) + mod_ref[0:1, :]).astype(jnp.bfloat16)

    features = HEADS * HEAD
    left = lax.broadcasted_iota(jnp.int32, (rows, LANES), 1) < HEAD
    loads[0].wait()

    def project(at_col):
        return jnp.dot(
            adapted[...], qkv_w[:, at_col : at_col + features], preferred_element_type=jnp.float32
        )

    def tile(array, i):
        return array[:, i * LANES : (i + 1) * LANES]

    def lone(array, g):
        held = tile(array, SPLIT + g // 2)
        return held if g % 2 == 0 else pltpu.roll(held, HEAD, 1)

    def lone_right(array, g):
        held = tile(array, SPLIT + g // 2)
        return held if g % 2 == 1 else pltpu.roll(held, HEAD, 1)

    key = project(features)
    value = project(2 * features)
    for g in range(SPLIT):
        pack[g, :, 0:LANES] = tile(key, g).astype(jnp.bfloat16)
        pack[g, :, LANES : 2 * LANES] = jnp.where(left, lone(key, g), lone_right(value, g)).astype(jnp.bfloat16)
        pack[g, :, 2 * LANES : 3 * LANES] = tile(value, g).astype(jnp.bfloat16)

    def spot(e, d, par):
        first = ((d * pairs + e) * 2 + par) * rows
        return kvb.at[pl.ds(first, rows), :]

    for d in range(1, SPLIT):
        send(pack.at[flip(hh, d)], spot(0, d, 0), kz_s.at[d], kz_r.at[d], zmate[d])
    kvb[0:rows, :] = pack[hh]

    def relay_kv(d):
        for f in range(1, pairs):
            send(spot(0, d, 0), spot(pairs - f, d, 0), ky_s.at[f, d], ky_r.at[f, d], ymate[f])
        send(spot(0, d, 0), spot(0, d, 1), kc_s.at[0, d], kc_r.at[0, d], sibling)

    relay_kv(0)

    query = project(0) * (1.0 / HEAD**0.5)
    for g in range(SPLIT):
        qpack[g, :, 0:LANES] = tile(query, g).astype(jnp.bfloat16)
        qpack[g, :, LANES : 2 * LANES] = jnp.where(left, lone(query, g), 0.0).astype(jnp.bfloat16)
    for d in range(1, SPLIT):
        send(qpack.at[flip(hh, d)], qbuf.at[d], q_s.at[d], q_r.at[d], zmate[d])
    qbuf[0] = qpack[hh]

    m_ref[...] = jnp.full_like(m_ref, -1e30)
    l_ref[...] = jnp.zeros_like(l_ref)
    acc_ref[...] = jnp.zeros_like(acc_ref)

    for d in range(1, SPLIT):
        arrive(spot(0, d, 0), kz_s.at[d], kz_r.at[d])
        relay_kv(d)
    for d in range(SPLIT):
        for e in range(1, pairs):
            f = pairs - e
            arrive(spot(e, d, 0), ky_s.at[f, d], ky_r.at[f, d])
            send(spot(e, d, 0), spot(e, d, 1), kc_s.at[e, d], kc_r.at[e, d], sibling)
    for d in range(1, SPLIT):
        arrive(qbuf.at[d], q_s.at[d], q_r.at[d])

    keys = members * rows
    for d in range(SPLIT):
        for e in range(pairs):
            arrive(spot(e, d, 1), kc_s.at[e, d], kc_r.at[e, d])

        @pl.loop(0, SPLIT)
        def _(t):
            for h in range(3):
                if h < 2:
                    q = qbuf[t, :, 0:LANES]
                    q = jnp.where(left if h == 0 else ~left, q, jnp.zeros_like(q))
                else:
                    q = qbuf[t, :, LANES : 2 * LANES]
                kt, vt = (0, 2) if h < 2 else (1, 1)
                k = kvb[d * keys : (d + 1) * keys, kt * LANES : (kt + 1) * LANES]
                v = kvb[d * keys : (d + 1) * keys, vt * LANES : (vt + 1) * LANES]
                scores = lax.dot_general(
                    q, k, (((1,), (1,)), ((), ())), preferred_element_type=jnp.float32
                )
                best = m_ref[h, t]
                new_best = jnp.maximum(best, jnp.max(scores, axis=-1, keepdims=True))
                shrink = jnp.exp(best - new_best)
                expo = jnp.exp(scores - new_best[:, 0:1])
                part = expo[:, 0:LANES]
                for i in range(1, keys // LANES):
                    part = part + expo[:, i * LANES : (i + 1) * LANES]
                m_ref[h, t] = new_best
                l_ref[h, t] = l_ref[h, t] * shrink + part
                acc_ref[h, t] = acc_ref[h, t] * shrink + jnp.dot(
                    expo.astype(jnp.bfloat16), v, preferred_element_type=jnp.float32
                )

    for t in range(SPLIT):
        mixed = [acc_ref[h, t] / jnp.sum(l_ref[h, t], axis=-1, keepdims=True) for h in range(3)]
        osend[t, :, 0:LANES] = jnp.where(left, mixed[0], mixed[1]).astype(jnp.bfloat16)
        osend[t, :, LANES : 2 * LANES] = mixed[2].astype(jnp.bfloat16)
        if t > 0:
            send(osend.at[t], obuf.at[hh], o_s.at[t], o_r.at[t], zmate[t])
    obuf[hh] = osend[0]
    for d in range(1, SPLIT):
        arrive(obuf.at[flip(hh, d)], o_s.at[d], o_r.at[d])
    loads[1].wait()

    parts = [obuf[g, :, 0:LANES] for g in range(SPLIT)]
    for g in range(0, SPLIT, 2):
        first = pltpu.roll(obuf[g, :, LANES : 2 * LANES].astype(jnp.float32), HEAD, 1)
        second = obuf[g + 1, :, LANES : 2 * LANES].astype(jnp.float32)
        parts.append(jnp.where(left, first, second).astype(jnp.bfloat16))
    attended = jnp.concatenate(parts, axis=1)
    projected_out = jnp.dot(attended, out_w[...], preferred_element_type=jnp.float32)
    result_ref[...] = (hidden[...].astype(jnp.float32) + mod_ref[2:3, :] * projected_out).astype(jnp.bfloat16)

    for copy in sent:
        copy.wait_send()


def per_device(n, groups, tokens, control, zero_weight, modulation, qkv_weight, out_weight):
    rows, width = tokens.shape
    cols = zero_weight.shape[1]
    members = n // SPLIT
    pairs = members // 2
    span = n // VIEWS
    gather = groups == 2 and cols % 48 == 0
    weight = zero_weight
    if not gather:
        weight = lax.all_gather(jnp.transpose(zero_weight), "seq", axis=0, tiled=True)
    vmem = pl.BlockSpec(memory_space=pltpu.VMEM)
    anywhere = pl.BlockSpec(memory_space=pl.ANY)
    bf16, f32, dma = jnp.bfloat16, jnp.float32, pltpu.SemaphoreType.DMA
    features = HEADS * HEAD
    return pl.pallas_call(
        functools.partial(kernel, n, gather),
        out_shape=jax.ShapeDtypeStruct((rows, width), bf16),
        in_specs=[vmem, vmem, vmem if gather else anywhere, vmem, anywhere, anywhere],
        out_specs=vmem,
        scratch_shapes=[
            pltpu.VMEM((width, width), bf16),
            pltpu.VMEM(qkv_weight.shape, bf16),
            pltpu.VMEM(out_weight.shape, bf16),
            pltpu.VMEM((span, 2, 8, LANES), f32),
            pltpu.VMEM((rows, width), bf16),
            pltpu.VMEM((rows, width), bf16),
            pltpu.VMEM((SPLIT, rows, 3 * LANES), bf16),
            pltpu.VMEM((SPLIT, rows, 2 * LANES), bf16),
            pltpu.VMEM((n * rows, 3 * LANES), bf16),
            pltpu.VMEM((SPLIT, rows, 2 * LANES), bf16),
            pltpu.VMEM((SPLIT, rows, 2 * LANES), bf16),
            pltpu.VMEM((SPLIT, rows, 2 * LANES), bf16),
            pltpu.VMEM((3, SPLIT, rows, LANES), f32),
            pltpu.VMEM((3, SPLIT, rows, LANES), f32),
            pltpu.VMEM((3, SPLIT, rows, LANES), f32),
            dma((3,)),
            dma((span,)),
            dma((span,)),
            dma((SPLIT,)),
            dma((SPLIT,)),
            dma((pairs, SPLIT)),
            dma((pairs, SPLIT)),
            dma((pairs, SPLIT)),
            dma((pairs, SPLIT)),
            dma((2, pairs, SPLIT)),
            dma((2, pairs, SPLIT)),
            dma((SPLIT,)),
            dma((SPLIT,)),
            dma((pairs, SPLIT)),
            dma((pairs, SPLIT)),
            dma((pairs, SPLIT)),
            dma((pairs, SPLIT)),
            dma((SPLIT,)),
            dma((SPLIT,)),
            dma((SPLIT,)),
            dma((SPLIT,)),
        ],
        compiler_params=pltpu.CompilerParams(
            collective_id=0, has_side_effects=True, vmem_limit_bytes=56 * 1024 * 1024
        ),
    )(tokens, control, weight, modulation, qkv_weight, out_weight)


def solution(mesh):
    placed = (
        P(("groups", "seq"), None),
        P(("groups", "seq"), None),
        P(None, "seq"),
        P("groups", None),
        P(),
        P(),
    )
    return jax.shard_map(
        functools.partial(per_device, mesh.shape["seq"], mesh.shape["groups"]),
        mesh=mesh,
        in_specs=placed,
        out_specs=P(("groups", "seq"), None),
        check_vma=False,
    )
```

time: 193 us -> 83.1 us (0.43)
  Pallas kernels: 0 us -> 79.2 us
  waiting for transfers between devices: 73.8 us -> 0 us
  blocking collectives: 65 us -> 0 us
  matrix products: 19 us -> 0 us
  between operations: 13.2 us -> 0.01 us
  local copies, waits for them, and re-layouts: 15.4 us -> 3.65 us
  other arithmetic: 6.37 us -> 0 us
    pallas_call x0 -> x1, Pallas kernels: none -> 79.2 us  [per_device(): pl.pallas_call(functools.partial(kernel, n, gather), out_shape=jax.ShapeD...]
    all_gather x3 -> x0, waiting for transfers between devices: 72.4 us -> none  [the longest x1 41.6 us: per_device(): lax.all_gather(key_local, 'seq', axis=0, tiled=True)]
    psum x2 -> x0, blocking collectives: 65 us -> none  [the longest x1 35.2 us: per_device(): mean_table = lax.psum(picker * local_sums[None, :], 'seq')]
    dot_general x5 -> x0, matrix products: 19 us -> none  [the longest x1 8.27 us: absorb(): jnp.einsum('hqk,khd->qhd', expo.astype(jnp.bfloat16), value_piece.reshape...]
    all_gather x2 -> x0, local copies, waits for them, and re-layouts: 9.42 us -> none  [the longest x1 4.71 us: per_device(): lax.all_gather(value_local, 'seq', axis=0, tiled=True)]
    reduce_sum x8 -> x0, other arithmetic: 5.26 us -> none  [the longest x1 2.44 us: absorb(): total = jnp.sum(expo, axis=-1)]
    unnamed x6 -> x2, local copies, waits for them, and re-layouts: 4.56 us -> 3.65 us
  transfers between devices with their start and end apart: 3 -> 0, of which waited for: 2 -> 0; matrix products, arithmetic and copies ran while one was open for 8% -> 0% of each run, Pallas kernels for 0% -> 0%
where the time goes in v1:
time: 83.1 us; the launch traced here: 82.9 us
  Pallas kernels  79.2 us (95%)
  local copies, waits for them, and re-layouts  3.65 us (4%)
    pallas_call x1, Pallas kernels, per_device(): pl.pallas_call(functools.partial(kernel, n, gather), out_shape=jax.ShapeD...  79.2 us
    unnamed x2, local copies, waits for them, and re-layouts  3.65 us

profile of v1, /device:TPU:0, one launch (start us, length us, event | category | flops | bytes accessed | tf_op | source)
XLA Modules:
  0.0 82.9 jit_solution(1584900914789014996)
XLA Ops:
  0.0 1.9 %copy.7.w_ref = bf16[1536,96]{1,0:T(8,128)(2,1)} copy(bf16[1536,96]{0,1:T(8,128)(2,1)} %param.8) | data formatting | bytes 589824 | tf_op args[2]
  1.9 79.2 %shard_map.64 = bf16[128,1536]{1,0:T(8,128)(2,1)} custom-call(bf16[128,1536]{1,0:T(8,128)(2,1)} %tokens_ref.1, bf16[128,1536]{1,0:T(8,128)(2,1)} %control_ref.1, bf16[1536,96]{1,0:T(8,128)(2,1)} %copy.7.w_ref, f32[3,1536]{1,0:T(4,128)} %mod_ref.1, bf16[1536,2304]{1,0:T(8,128)(2,1)} %qkv_hbm.1, bf16[768,1536]{1,0:T(8,128)(2,1)} %out_hbm.1), custom_call_target="tpu_custom_call" | custom-call | tf_op jit(solution)/shard_map/pallas_call | solution.py:394
  81.1 1.8 %copy.9 = bf16[128,1536]{1,0:T(8,128)(2,1)} copy(bf16[128,1536]{1,0:T(8,128)(2,1)} %shard_map.64) | data formatting | bytes 786432

commit v2 on v1

v2 whole, which is shorter than its diff:
```python
import functools

import jax
import jax.numpy as jnp
from jax import lax
from jax.experimental import pallas as pl
from jax.experimental.pallas import tpu as pltpu
from jax.sharding import PartitionSpec as P

HEADS = 12
HEAD = 64
GROUPS = 32
VIEWS = 8
QUERY_TILE = 256
SPLIT = 4
LANES = 128
MESH = pl.DeviceIdType.MESH


def flip(index, d):
    if d == 0:
        return index
    if d == 1:
        return index + 1 - 2 * (index % 2)
    if d == 2:
        return index + 2 - 4 * (index // 2)
    return 3 - index


def kernel(
    n,
    gather,
    tokens_hbm,
    control_hbm,
    w_hbm,
    mod_ref,
    qkv_hbm,
    out_hbm,
    result_ref,
    tokens_ref,
    control_ref,
    wbuf,
    nbuf,
    rbuf,
    mine,
    theirs,
    qkv_w,
    out_w,
    stat,
    hidden,
    adapted,
    pack,
    qpack,
    kvb,
    qbuf,
    obuf,
    osend,
    m_ref,
    l_ref,
    acc_ref,
    load_sem,
    stat_s,
    stat_r,
    wz_s,
    wz_r,
    ny_s,
    ny_r,
    ry_s,
    ry_r,
    wx_s,
    wx_r,
    wc_s,
    wc_r,
    kz_s,
    kz_r,
    ky_s,
    ky_r,
    kc_s,
    kc_r,
    q_s,
    q_r,
    o_s,
    o_r,
):
    rows, width = tokens_hbm.shape
    per_group = width // GROUPS
    cols = width // n
    members = n // SPLIT
    pairs = members // 2
    span = n // VIEWS
    me_g = lax.axis_index("groups")
    me = lax.axis_index("seq")
    hh = me // members
    uu = (me % members) // 2
    cc = me % 2

    def at(h, u, c):
        return (me_g, (h * pairs + u) * 2 + c)

    sibling = at(hh, uu, 1 - cc)
    zmate = [at(flip(hh, d), uu, cc) for d in range(SPLIT)]
    ymate = [at(hh, (uu + f) % pairs, cc) for f in range(pairs)]
    xmate = (1 - me_g, me)
    view_base = (me // span) * span
    peer = [(me_g, view_base + (me - view_base + f) % span) for f in range(span)]

    loads = [
        pltpu.make_async_copy(qkv_hbm, qkv_w, load_sem.at[0]),
        pltpu.make_async_copy(out_hbm, out_w, load_sem.at[1]),
        pltpu.make_async_copy(control_hbm, control_ref, load_sem.at[2]),
        pltpu.make_async_copy(tokens_hbm, tokens_ref, load_sem.at[3]),
    ]
    loads = [loads[2], loads[3], loads[0], loads[1]]
    load_control, load_tokens, load_qkv, load_out = loads
    if gather:
        place = pl.ds(pl.multiple_of((hh * 2 + cc) * cols, cols), cols)
        load_w = pltpu.make_async_copy(w_hbm, wbuf.at[place, :], load_sem.at[4])
    else:
        load_w = pltpu.make_async_copy(w_hbm, wbuf, load_sem.at[4])
    loads.append(load_w)
    for load in loads:
        load.start()

    barrier = pltpu.get_barrier_semaphore()
    greet = [sibling] + zmate[1:] + ymate[1:] + peer[1:] + ([xmate] if gather else [])
    for device in greet:
        pl.semaphore_signal(barrier, inc=1, device_id=device, device_id_type=MESH)

    pl.semaphore_wait(barrier, len(greet))

    sent = []

    def send(src, dst, ssem, rsem, device):
        copy = pltpu.make_async_remote_copy(
            src_ref=src, dst_ref=dst, send_sem=ssem, recv_sem=rsem, device_id=device, device_id_type=MESH
        )
        copy.start()
        sent.append(copy)

    def arrive(dst, ssem, rsem):
        pltpu.make_async_remote_copy(
            src_ref=dst, dst_ref=dst, send_sem=ssem, recv_sem=rsem, device_id=sibling, device_id_type=MESH
        ).wait_recv()

    half = cols // 2
    plane = half * me_g
    from_x = half * (1 - me_g)

    def slab(d, c, start, count):
        owner = flip(hh, d) * 2 + c
        return wbuf.at[pl.ds(pl.multiple_of(owner * cols + start, half), count), :]

    if gather:
        own = w_hbm.at[pl.ds(pl.multiple_of(plane, half), half), :]
        for d in range(1, SPLIT):
            send(own, slab(0, cc, plane, half), wz_s.at[d], wz_r.at[d], zmate[d])
        send(w_hbm, slab(0, cc, 0, cols), wc_s.at[0, 0], wc_r.at[0, 0], sibling)

    lane_group = lax.broadcasted_iota(jnp.int32, (width, LANES), 1) * per_group
    channel = lax.broadcasted_iota(jnp.int32, (width, LANES), 0)
    member = ((channel >= lane_group) & (channel < lane_group + per_group)).astype(jnp.float32)

    member = member.astype(jnp.bfloat16)

    def thirds(line):
        high = line.astype(jnp.bfloat16).astype(jnp.float32)
        rest = line - high
        middle = rest.astype(jnp.bfloat16).astype(jnp.float32)
        return [high, middle, rest - middle]

    def stack(lines):
        wide = lines[0].shape[1]
        lines = lines + [jnp.zeros((16 - len(lines), wide), jnp.float32)]
        return jnp.concatenate(lines, axis=0).astype(jnp.bfloat16)

    def group_sum(line):
        sums = jnp.dot(stack(thirds(line)), member, preferred_element_type=jnp.float32)
        return sums[0:1] + sums[1:2] + sums[2:3]

    def spread(*lines):
        split = [part for line in lines for part in thirds(line)]
        wide = lax.dot_general(
            stack(split), member, (((1,), (1,)), ((), ())), preferred_element_type=jnp.float32
        )
        return [wide[i : i + 1] + wide[i + 1 : i + 2] + wide[i + 2 : i + 3] for i in range(0, len(split), 3)]

    load_control.wait()
    local_count = float(rows * per_group)
    control_f = control_ref[...].astype(jnp.float32)
    col_sum = jnp.sum(control_f, axis=0, keepdims=True)
    local_mean = group_sum(col_sum) / local_count
    off = control_f - spread(local_mean)[0]
    col_sq = jnp.sum(off * off, axis=0, keepdims=True)
    local_m2 = group_sum(col_sq)
    stat[0, 0] = jnp.broadcast_to(local_mean, (8, LANES))
    stat[0, 1] = jnp.broadcast_to(local_m2, (8, LANES))
    for f in range(1, span):
        send(stat.at[0], stat.at[f], stat_s.at[f], stat_r.at[f], peer[f])
    for f in range(1, span):
        arrive(stat.at[f], stat_s.at[f], stat_r.at[f])
    mean = stat[0, 0, 0:1]
    m2 = stat[0, 1, 0:1]
    for f in range(1, span):
        mean = mean + stat[f, 0, 0:1]
        m2 = m2 + stat[f, 1, 0:1]
    mean = mean / span
    for f in range(span):
        gap = stat[f, 0, 0:1] - mean
        m2 = m2 + local_count * (gap * gap)
    var = m2 / (local_count * span)
    inv = 1.0 / jnp.sqrt(var + 1e-05)
    mean_line, inv_line = spread(mean, inv)
    nbuf[0:rows, :] = ((control_ref[...].astype(jnp.float32) - mean_line) * inv_line).astype(jnp.bfloat16)
    if gather:
        send(nbuf.at[0:rows, :], nbuf.at[rows : 2 * rows, :], ny_s, ny_r, ymate[1])
    load_tokens.wait()

    if gather:
        half_block = width // 4

        def multiply(p):
            place = pl.ds(pl.multiple_of(p * half_block, half_block), half_block)
            residual = lax.dot_general(
                nbuf[...], wbuf[place, :], (((1,), (1,)), ((), ())), preferred_element_type=jnp.float32
            )
            mine[p] = residual[0:rows]
            theirs[p] = residual[rows : 2 * rows].astype(jnp.bfloat16)

        load_w.wait()
        for d in range(1, SPLIT):
            part = slab(d, cc, plane, half)
            arrive(part, wz_s.at[d], wz_r.at[d])
            send(part, part, wx_s.at[d], wx_r.at[d], xmate)
            send(part, part, wc_s.at[0, d], wc_r.at[0, d], sibling)
        for d in range(1, SPLIT):
            part = slab(d, cc, from_x, half)
            arrive(part, wx_s.at[d], wx_r.at[d])
            send(part, part, wc_s.at[1, d], wc_r.at[1, d], sibling)
        arrive(nbuf.at[rows : 2 * rows, :], ny_s, ny_r)
        arrive(slab(0, 1 - cc, 0, cols), wc_s.at[0, 0], wc_r.at[0, 0])
        for step in range(2):
            for d in range(2 * step, 2 * step + 2):
                if d > 0:
                    arrive(slab(d, 1 - cc, plane, half), wc_s.at[0, d], wc_r.at[0, d])
                    arrive(slab(d, 1 - cc, from_x, half), wc_s.at[1, d], wc_r.at[1, d])
            place = flip(hh // 2, step)
            multiply(place)
            send(theirs.at[place], rbuf.at[place], ry_s.at[step], ry_r.at[step], ymate[1])
        for step in range(2):
            place = flip(hh // 2, step)
            arrive(rbuf.at[place], ry_s.at[step], ry_r.at[step])
        for p in range(2):
            got = rbuf[p].astype(jnp.float32)
            low = jnp.where(uu == 0, mine[p], got)
            high = jnp.where(uu == 0, got, mine[p])
            cut = half_block // 2
            residual = jnp.concatenate([low[:, :cut], high[:, :cut], low[:, cut:], high[:, cut:]], axis=1)
            place = slice(2 * p * half_block, 2 * (p + 1) * half_block)
            hidden[:, place] = (tokens_ref[:, place].astype(jnp.float32) + residual).astype(jnp.bfloat16)
    else:
        load_w.wait()
        residual = lax.dot_general(
            nbuf[0:rows, :], wbuf[...], (((1,), (1,)), ((), ())), preferred_element_type=jnp.float32
        )
        hidden[...] = (tokens_ref[...].astype(jnp.float32) + residual).astype(jnp.bfloat16)

    hidden_f = hidden[...].astype(jnp.float32)
    tok_mean = jnp.mean(hidden_f, axis=-1, keepdims=True)
    tok_dev = hidden_f - tok_mean
    tok_var = jnp.mean(tok_dev * tok_dev, axis=-1, keepdims=True)
    layered = tok_dev / jnp.sqrt(tok_var + 1e-06)
    adapted[...] = (layered * (1.0 + mod_ref[1:2, :]) + mod_ref[0:1, :]).astype(jnp.bfloat16)

    features = HEADS * HEAD
    left = lax.broadcasted_iota(jnp.int32, (rows, LANES), 1) < HEAD
    load_qkv.wait()

    def project(at_col):
        return jnp.dot(
            adapted[...], qkv_w[:, at_col : at_col + features], preferred_element_type=jnp.float32
        )

    def tile(array, i):
        return array[:, i * LANES : (i + 1) * LANES]

    def lone(array, g):
        held = tile(array, SPLIT + g // 2)
        return held if g % 2 == 0 else pltpu.roll(held, HEAD, 1)

    def lone_right(array, g):
        held = tile(array, SPLIT + g // 2)
        return held if g % 2 == 1 else pltpu.roll(held, HEAD, 1)

    query = project(0) * (1.0 / HEAD**0.5)
    for g in range(SPLIT):
        qpack[g, :, 0:LANES] = tile(query, g).astype(jnp.bfloat16)
        qpack[g, :, LANES : 2 * LANES] = jnp.where(left, lone(query, g), 0.0).astype(jnp.bfloat16)
    def qpart(d):
        return qbuf.at[pl.ds(d * rows, rows), :]

    for d in range(1, SPLIT):
        send(qpack.at[flip(hh, d)], qpart(d), q_s.at[d], q_r.at[d], zmate[d])
    qbuf[0:rows, :] = qpack[hh]

    key = project(features)
    value = project(2 * features)
    for g in range(SPLIT):
        pack[g, :, 0:LANES] = tile(key, g).astype(jnp.bfloat16)
        pack[g, :, LANES : 2 * LANES] = jnp.where(left, lone(key, g), lone_right(value, g)).astype(jnp.bfloat16)
        pack[g, :, 2 * LANES : 3 * LANES] = tile(value, g).astype(jnp.bfloat16)

    def spot(e, d, par):
        first = ((e * SPLIT + d) * 2 + par) * rows
        return kvb.at[pl.ds(first, rows), :]

    for d in range(1, SPLIT):
        send(pack.at[flip(hh, d)], spot(0, d, 0), kz_s.at[d], kz_r.at[d], zmate[d])
    kvb[0:rows, :] = pack[hh]

    def relay_kv(d):
        for f in range(1, pairs):
            send(spot(0, d, 0), spot(pairs - f, d, 0), ky_s.at[f, d], ky_r.at[f, d], ymate[f])
        send(spot(0, d, 0), spot(0, d, 1), kc_s.at[0, d], kc_r.at[0, d], sibling)

    def take_z(d):
        arrive(spot(0, d, 0), kz_s.at[d], kz_r.at[d])
        relay_kv(d)

    def take_y(e, d):
        f = pairs - e
        arrive(spot(e, d, 0), ky_s.at[f, d], ky_r.at[f, d])
        send(spot(e, d, 0), spot(e, d, 1), kc_s.at[e, d], kc_r.at[e, d], sibling)

    def take_c(e, part):
        for d in (2 * part, 2 * part + 1):
            arrive(spot(e, d, 1), kc_s.at[e, d], kc_r.at[e, d])

    keys = SPLIT * rows
    deep = QUERY_TILE
    left_q = lax.broadcasted_iota(jnp.int32, (deep, LANES), 1) < HEAD

    def absorb(at_row, e, part):
        first = (2 * e + part) * keys
        mine_q = pl.ds(at_row, deep)
        for h in range(3):
            if h < 2:
                q = qbuf[mine_q, 0:LANES]
                q = jnp.where(left_q if h == 0 else ~left_q, q, jnp.zeros_like(q))
            else:
                q = qbuf[mine_q, LANES : 2 * LANES]
            kt, vt = (0, 2) if h < 2 else (1, 1)
            k = kvb[first : first + keys, kt * LANES : (kt + 1) * LANES]
            v = kvb[first : first + keys, vt * LANES : (vt + 1) * LANES]
            scores = lax.dot_general(q, k, (((1,), (1,)), ((), ())), preferred_element_type=jnp.float32)
            tiles = [scores[:, i : i + LANES] for i in range(0, keys, LANES)]
            top = functools.reduce(jnp.maximum, tiles)
            top = jnp.broadcast_to(jnp.max(top, axis=-1, keepdims=True), top.shape)
            fresh = (e, part) == (0, 0)
            if not fresh:
                best = m_ref[h, mine_q, :]
                top = jnp.maximum(best, top)
                shrink = jnp.exp(best - top)
            m_ref[h, mine_q, :] = top
            expo = [jnp.exp(x - top) for x in tiles]
            total = functools.reduce(jnp.add, expo)
            probs = jnp.concatenate([x.astype(jnp.bfloat16) for x in expo], axis=1)
            mixed = jnp.dot(probs, v, preferred_element_type=jnp.float32)
            if not fresh:
                total = total + l_ref[h, mine_q, :] * shrink
                mixed = mixed + acc_ref[h, mine_q, :] * shrink
            l_ref[h, mine_q, :] = total
            acc_ref[h, mine_q, :] = mixed

    def absorb_all(e, part):
        @pl.loop(0, SPLIT * rows // deep)
        def _(t):
            absorb(pl.multiple_of(t * deep, deep), e, part)

    relay_kv(0)
    for d in range(1, SPLIT):
        arrive(qpart(d), q_s.at[d], q_r.at[d])
    take_z(1)
    take_c(0, 0)
    absorb_all(0, 0)
    for e in range(1, pairs):
        take_y(e, 0)
        take_y(e, 1)
        take_c(e, 0)
        absorb_all(e, 0)
    take_z(2)
    take_z(3)
    take_c(0, 1)
    absorb_all(0, 1)
    for e in range(1, pairs):
        take_y(e, 2)
        take_y(e, 3)
    for e in range(1, pairs):
        take_c(e, 1)
        if e < pairs - 1:
            absorb_all(e, 1)

    for at_row in reversed(range(0, SPLIT * rows, deep)):
        if pairs > 1:
            absorb(at_row, pairs - 1, 1)
        for t in range(at_row // rows, (at_row + deep) // rows):
            q_rows = slice(t * rows, (t + 1) * rows)
            mixed = [
                acc_ref[h, q_rows, :] / jnp.sum(l_ref[h, q_rows, :], axis=-1, keepdims=True) for h in range(3)
            ]
            osend[t, :, 0:LANES] = jnp.where(left, mixed[0], mixed[1]).astype(jnp.bfloat16)
            osend[t, :, LANES : 2 * LANES] = mixed[2].astype(jnp.bfloat16)
            if t > 0:
                send(osend.at[t], obuf.at[hh], o_s.at[t], o_r.at[t], zmate[t])
    obuf[hh] = osend[0]
    for d in range(1, SPLIT):
        arrive(obuf.at[flip(hh, d)], o_s.at[d], o_r.at[d])
    load_out.wait()

    parts = [obuf[g, :, 0:LANES] for g in range(SPLIT)]
    for g in range(0, SPLIT, 2):
        first = pltpu.roll(obuf[g, :, LANES : 2 * LANES].astype(jnp.float32), HEAD, 1)
        second = obuf[g + 1, :, LANES : 2 * LANES].astype(jnp.float32)
        parts.append(jnp.where(left, first, second).astype(jnp.bfloat16))
    attended = jnp.concatenate(parts, axis=1)
    projected_out = jnp.dot(attended, out_w[...], preferred_element_type=jnp.float32)
    result_ref[...] = (hidden[...].astype(jnp.float32) + mod_ref[2:3, :] * projected_out).astype(jnp.bfloat16)

    for copy in sent:
        copy.wait_send()


def per_device(n, groups, tokens, control, zero_weight, modulation, qkv_weight, out_weight):
    rows, width = tokens.shape
    cols = zero_weight.shape[1]
    members = n // SPLIT
    pairs = members // 2
    span = n // VIEWS
    gather = groups == 2 and pairs == 2 and cols % 96 == 0
    weight = jnp.transpose(zero_weight)
    if not gather:
        weight = lax.all_gather(weight, "seq", axis=0, tiled=True)
    vmem = pl.BlockSpec(memory_space=pltpu.VMEM)
    anywhere = pl.BlockSpec(memory_space=pl.ANY)
    bf16, f32, dma = jnp.bfloat16, jnp.float32, pltpu.SemaphoreType.DMA
    features = HEADS * HEAD
    return pl.pallas_call(
        functools.partial(kernel, n, gather),
        out_shape=jax.ShapeDtypeStruct((rows, width), bf16),
        in_specs=[anywhere, anywhere, anywhere, vmem, anywhere, anywhere],
        out_specs=vmem,
        scratch_shapes=[
            pltpu.VMEM((rows, width), bf16),
            pltpu.VMEM((rows, width), bf16),
            pltpu.VMEM((width // 2 if gather else width, width), bf16),
            pltpu.VMEM((2 * rows, width), bf16),
            pltpu.VMEM((2, rows, width // 4), bf16),
            pltpu.VMEM((2, rows, width // 4), f32),
            pltpu.VMEM((2, rows, width // 4), bf16),
            pltpu.VMEM(qkv_weight.shape, bf16),
            pltpu.VMEM(out_weight.shape, bf16),
            pltpu.VMEM((span, 2, 8, LANES), f32),
            pltpu.VMEM((rows, width), bf16),
            pltpu.VMEM((rows, width), bf16),
            pltpu.VMEM((SPLIT, rows, 3 * LANES), bf16),
            pltpu.VMEM((SPLIT, rows, 2 * LANES), bf16),
            pltpu.VMEM((n * rows, 3 * LANES), bf16),
            pltpu.VMEM((SPLIT * rows, 2 * LANES), bf16),
            pltpu.VMEM((SPLIT, rows, 2 * LANES), bf16),
            pltpu.VMEM((SPLIT, rows, 2 * LANES), bf16),
            pltpu.VMEM((3, SPLIT * rows, LANES), f32),
            pltpu.VMEM((3, SPLIT * rows, LANES), f32),
            pltpu.VMEM((3, SPLIT * rows, LANES), f32),
            dma((5,)),
            dma((span,)),
            dma((span,)),
            dma((SPLIT,)),
            dma((SPLIT,)),
            dma(()),
            dma(()),
            dma((2,)),
            dma((2,)),
            dma((SPLIT,)),
            dma((SPLIT,)),
            dma((2, SPLIT)),
            dma((2, SPLIT)),
            dma((SPLIT,)),
            dma((SPLIT,)),
            dma((pairs, SPLIT)),
            dma((pairs, SPLIT)),
            dma((pairs, SPLIT)),
            dma((pairs, SPLIT)),
            dma((SPLIT,)),
            dma((SPLIT,)),
            dma((SPLIT,)),
            dma((SPLIT,)),
        ],
        compiler_params=pltpu.CompilerParams(
            collective_id=0, has_side_effects=True, vmem_limit_bytes=56 * 1024 * 1024
        ),
    )(tokens, control, weight, modulation, qkv_weight, out_weight)


def solution(mesh):
    placed = (
        P(("groups", "seq"), None),
        P(("groups", "seq"), None),
        P(None, "seq"),
        P("groups", None),
        P(),
        P(),
    )
    return jax.shard_map(
        functools.partial(per_device, mesh.shape["seq"], mesh.shape["groups"]),
        mesh=mesh,
        in_specs=placed,
        out_specs=P(("groups", "seq"), None),
        check_vma=False,
    )
```

time: 83.1 us -> 67.8 us (0.82)
  Pallas kernels: 79.2 us -> 65.8 us
  local copies, waits for them, and re-layouts: 3.65 us -> 1.77 us
    pallas_call x1, Pallas kernels: 79.2 us -> 65.8 us  [per_device(): pl.pallas_call(functools.partial(kernel, n, gather), out_shape=jax.ShapeD...]
    unnamed x2 -> x1, local copies, waits for them, and re-layouts: 3.65 us -> 1.77 us
where the time goes in v2:
time: 67.8 us; the launch traced here: 67.6 us
  Pallas kernels  65.8 us (97%)
  local copies, waits for them, and re-layouts  1.77 us (3%)
    pallas_call x1, Pallas kernels, per_device(): pl.pallas_call(functools.partial(kernel, n, gather), out_shape=jax.ShapeD...  65.8 us
    unnamed x1, local copies, waits for them, and re-layouts  1.77 us

profile of v2, /device:TPU:0, one launch (start us, length us, event | category | flops | bytes accessed | tf_op | source)
XLA Modules:
  0.0 67.6 jit_solution(11295186702883319684)
XLA Ops:
  0.0 65.8 %shard_map.64 = bf16[128,1536]{1,0:T(8,128)(2,1)} custom-call(bf16[128,1536]{1,0:T(8,128)(2,1)} %tokens_hbm.1, bf16[128,1536]{1,0:T(8,128)(2,1)} %control_hbm.1, bf16[96,1536]{1,0:T(8,128)(2,1)} %bitcast.1, f32[3,1536]{1,0:T(4,128)} %mod_ref.1, bf16[1536,2304]{1,0:T(8,128)(2,1)} %qkv_hbm.1, bf16[768,1536]{1,0:T(8,128)(2,1)} %out_hbm.1), custom_call_target="tpu_custom_call" | custom-call | tf_op jit(solution)/shard_map/pallas_call | solution.py:446
  65.8 1.8 %copy.8 = bf16[128,1536]{1,0:T(8,128)(2,1)} copy(bf16[128,1536]{1,0:T(8,128)(2,1)} %shard_map.64) | data formatting | bytes 786432

commit v3 on v2

--- a/solution.py
+++ b/solution.py
@@ -11,7 +11,8 @@
 HEAD = 64
 GROUPS = 32
 VIEWS = 8
-QUERY_TILE = 256
+EARLY_TILE = 512
+LAST_TILE = 256
 SPLIT = 4
 LANES = 128
 MESH = pl.DeviceIdType.MESH
@@ -52,6 +53,7 @@
     pack,
     qpack,
     kvb,
+    qin,
     qbuf,
     obuf,
     osend,
@@ -152,7 +154,7 @@
 
     if gather:
         own = w_hbm.at[pl.ds(pl.multiple_of(plane, half), half), :]
-        for d in range(1, SPLIT):
+        for d in range(1, SPLIT - 1):
             send(own, slab(0, cc, plane, half), wz_s.at[d], wz_r.at[d], zmate[d])
         send(w_hbm, slab(0, cc, 0, cols), wc_s.at[0, 0], wc_r.at[0, 0], sibling)
 
@@ -198,6 +200,8 @@
         send(stat.at[0], stat.at[f], stat_s.at[f], stat_r.at[f], peer[f])
     for f in range(1, span):
         arrive(stat.at[f], stat_s.at[f], stat_r.at[f])
+    if gather:
+        send(own, slab(0, cc, plane, half), wz_s.at[SPLIT - 1], wz_r.at[SPLIT - 1], zmate[SPLIT - 1])
     mean = stat[0, 0, 0:1]
     m2 = stat[0, 1, 0:1]
     for f in range(1, span):
@@ -291,16 +295,26 @@
         held = tile(array, SPLIT + g // 2)
         return held if g % 2 == 1 else pltpu.roll(held, HEAD, 1)
 
+    fold = rows // 2
     query = project(0) * (1.0 / HEAD**0.5)
     for g in range(SPLIT):
-        qpack[g, :, 0:LANES] = tile(query, g).astype(jnp.bfloat16)
-        qpack[g, :, LANES : 2 * LANES] = jnp.where(left, lone(query, g), 0.0).astype(jnp.bfloat16)
+        qpack[g, 0:rows, :] = tile(query, g).astype(jnp.bfloat16)
+        single = lone(query, g)
+        qpack[g, rows : rows + fold, :] = jnp.where(
+            left[:fold], single[:fold], pltpu.roll(single[fold:], HEAD, 1)
+        ).astype(jnp.bfloat16)
     def qpart(d):
-        return qbuf.at[pl.ds(d * rows, rows), :]
+        return qin.at[d]
+
+    def unfold_query(packed, d):
+        qbuf[d * rows : (d + 1) * rows, 0:LANES] = packed[0:rows]
+        single = packed[rows : rows + fold].astype(jnp.float32)
+        single = jnp.concatenate([single, pltpu.roll(single, HEAD, 1)], axis=0)
+        qbuf[d * rows : (d + 1) * rows, LANES : 2 * LANES] = jnp.where(left, single, 0.0).astype(jnp.bfloat16)
 
     for d in range(1, SPLIT):
         send(qpack.at[flip(hh, d)], qpart(d), q_s.at[d], q_r.at[d], zmate[d])
-    qbuf[0:rows, :] = qpack[hh]
+    unfold_query(qpack[hh], 0)
 
     key = project(features)
     value = project(2 * features)
@@ -313,8 +327,11 @@
         first = ((e * SPLIT + d) * 2 + par) * rows
         return kvb.at[pl.ds(first, rows), :]
 
-    for d in range(1, SPLIT):
+    def send_kv(d):
         send(pack.at[flip(hh, d)], spot(0, d, 0), kz_s.at[d], kz_r.at[d], zmate[d])
+
+    for d in range(1, SPLIT - 1):
+        send_kv(d)
     kvb[0:rows, :] = pack[hh]
 
     def relay_kv(d):
@@ -336,12 +353,11 @@
             arrive(spot(e, d, 1), kc_s.at[e, d], kc_r.at[e, d])
 
     keys = SPLIT * rows
-    deep = QUERY_TILE
-    left_q = lax.broadcasted_iota(jnp.int32, (deep, LANES), 1) < HEAD
-
-    def absorb(at_row, e, part):
+
+    def absorb(at_row, deep, e, part):
         first = (2 * e + part) * keys
         mine_q = pl.ds(at_row, deep)
+        left_q = lax.broadcasted_iota(jnp.int32, (deep, LANES), 1) < HEAD
         for h in range(3):
             if h < 2:
                 q = qbuf[mine_q, 0:LANES]
@@ -372,14 +388,16 @@
             acc_ref[h, mine_q, :] = mixed
 
     def absorb_all(e, part):
-        @pl.loop(0, SPLIT * rows // deep)
+        @pl.loop(0, SPLIT * rows // EARLY_TILE)
         def _(t):
-            absorb(pl.multiple_of(t * deep, deep), e, part)
+            absorb(pl.multiple_of(t * EARLY_TILE, EARLY_TILE), EARLY_TILE, e, part)
 
     relay_kv(0)
     for d in range(1, SPLIT):
         arrive(qpart(d), q_s.at[d], q_r.at[d])
+        unfold_query(qin[d], d)
     take_z(1)
+    send_kv(SPLIT - 1)
     take_c(0, 0)
     absorb_all(0, 0)
     for e in range(1, pairs):
@@ -399,16 +417,19 @@
         if e < pairs - 1:
             absorb_all(e, 1)
 
+    deep = LAST_TILE
     for at_row in reversed(range(0, SPLIT * rows, deep)):
         if pairs > 1:
-            absorb(at_row, pairs - 1, 1)
+            absorb(at_row, deep, pairs - 1, 1)
         for t in range(at_row // rows, (at_row + deep) // rows):
             q_rows = slice(t * rows, (t + 1) * rows)
             mixed = [
                 acc_ref[h, q_rows, :] / jnp.sum(l_ref[h, q_rows, :], axis=-1, keepdims=True) for h in range(3)
             ]
-            osend[t, :, 0:LANES] = jnp.where(left, mixed[0], mixed[1]).astype(jnp.bfloat16)
-            osend[t, :, LANES : 2 * LANES] = mixed[2].astype(jnp.bfloat16)
+            osend[t, 0:rows, :] = jnp.where(left, mixed[0], mixed[1]).astype(jnp.bfloat16)
+            osend[t, rows : rows + fold, :] = jnp.where(
+                left[:fold], pltpu.roll(mixed[2][:fold], HEAD, 1), mixed[2][fold:]
+            ).astype(jnp.bfloat16)
             if t > 0:
                 send(osend.at[t], obuf.at[hh], o_s.at[t], o_r.at[t], zmate[t])
     obuf[hh] = osend[0]
@@ -416,11 +437,13 @@
         arrive(obuf.at[flip(hh, d)], o_s.at[d], o_r.at[d])
     load_out.wait()
 
-    parts = [obuf[g, :, 0:LANES] for g in range(SPLIT)]
+    parts = [obuf[g, 0:rows, :] for g in range(SPLIT)]
     for g in range(0, SPLIT, 2):
-        first = pltpu.roll(obuf[g, :, LANES : 2 * LANES].astype(jnp.float32), HEAD, 1)
-        second = obuf[g + 1, :, LANES : 2 * LANES].astype(jnp.float32)
-        parts.append(jnp.where(left, first, second).astype(jnp.bfloat16))
+        first = obuf[g, rows : rows + fold, :].astype(jnp.float32)
+        second = obuf[g + 1, rows : rows + fold, :].astype(jnp.float32)
+        upper = jnp.where(left[:fold], first, pltpu.roll(second, HEAD, 1))
+        lower = jnp.where(left[:fold], pltpu.roll(first, HEAD, 1), second)
+        parts.append(jnp.concatenate([upper, lower], axis=0).astype(jnp.bfloat16))
     attended = jnp.concatenate(parts, axis=1)
     projected_out = jnp.dot(attended, out_w[...], preferred_element_type=jnp.float32)
     result_ref[...] = (hidden[...].astype(jnp.float32) + mod_ref[2:3, :] * projected_out).astype(jnp.bfloat16)
@@ -462,11 +485,12 @@
             pltpu.VMEM((rows, width), bf16),
             pltpu.VMEM((rows, width), bf16),
             pltpu.VMEM((SPLIT, rows, 3 * LANES), bf16),
-            pltpu.VMEM((SPLIT, rows, 2 * LANES), bf16),
+            pltpu.VMEM((SPLIT, rows + rows // 2, LANES), bf16),
             pltpu.VMEM((n * rows, 3 * LANES), bf16),
+            pltpu.VMEM((SPLIT, rows + rows // 2, LANES), bf16),
             pltpu.VMEM((SPLIT * rows, 2 * LANES), bf16),
-            pltpu.VMEM((SPLIT, rows, 2 * LANES), bf16),
-            pltpu.VMEM((SPLIT, rows, 2 * LANES), bf16),
+            pltpu.VMEM((SPLIT, rows + rows // 2, LANES), bf16),
+            pltpu.VMEM((SPLIT, rows + rows // 2, LANES), bf16),
             pltpu.VMEM((3, SPLIT * rows, LANES), f32),
             pltpu.VMEM((3, SPLIT * rows, LANES), f32),
             pltpu.VMEM((3, SPLIT * rows, LANES), f32),

time: 67.8 us -> 64.8 us (0.956)
  Pallas kernels: 65.8 us -> 62.8 us
    pallas_call x1, Pallas kernels: 65.8 us -> 62.8 us  [per_device(): pl.pallas_call(functools.partial(kernel, n, gather), out_shape=jax.ShapeD...]
where the time goes in v3:
time: 64.8 us; the launch traced here: 64.6 us
  Pallas kernels  62.8 us (97%)
  local copies, waits for them, and re-layouts  1.77 us (3%)
    pallas_call x1, Pallas kernels, per_device(): pl.pallas_call(functools.partial(kernel, n, gather), out_shape=jax.ShapeD...  62.8 us
    unnamed x1, local copies, waits for them, and re-layouts  1.77 us

profile of v3, /device:TPU:0, one launch (start us, length us, event | category | flops | bytes accessed | tf_op | source)
XLA Modules:
  0.0 64.6 jit_solution(3790179794231853578)
XLA Ops:
  0.0 62.8 %shard_map.64 = bf16[128,1536]{1,0:T(8,128)(2,1)} custom-call(bf16[128,1536]{1,0:T(8,128)(2,1)} %tokens_hbm.1, bf16[128,1536]{1,0:T(8,128)(2,1)} %control_hbm.1, bf16[96,1536]{1,0:T(8,128)(2,1)} %bitcast.1, f32[3,1536]{1,0:T(4,128)} %mod_ref.1, bf16[1536,2304]{1,0:T(8,128)(2,1)} %qkv_hbm.1, bf16[768,1536]{1,0:T(8,128)(2,1)} %out_hbm.1), custom_call_target="tpu_custom_call" | custom-call | tf_op jit(solution)/shard_map/pallas_call | solution.py:469
  62.8 1.8 %copy.8 = bf16[128,1536]{1,0:T(8,128)(2,1)} copy(bf16[128,1536]{1,0:T(8,128)(2,1)} %shard_map.64) | data formatting | bytes 786432

commit v4 on v3

--- a/solution.py
+++ b/solution.py
@@ -12,7 +12,7 @@
 GROUPS = 32
 VIEWS = 8
 EARLY_TILE = 512
-LAST_TILE = 256
+LAST_TILE = 128
 SPLIT = 4
 LANES = 128
 MESH = pl.DeviceIdType.MESH
@@ -236,13 +236,18 @@
             arrive(part, wz_s.at[d], wz_r.at[d])
             send(part, part, wx_s.at[d], wx_r.at[d], xmate)
             send(part, part, wc_s.at[0, d], wc_r.at[0, d], sibling)
-        for d in range(1, SPLIT):
+        def take_x(d):
             part = slab(d, cc, from_x, half)
             arrive(part, wx_s.at[d], wx_r.at[d])
             send(part, part, wc_s.at[1, d], wc_r.at[1, d], sibling)
+
+        take_x(1)
         arrive(nbuf.at[rows : 2 * rows, :], ny_s, ny_r)
         arrive(slab(0, 1 - cc, 0, cols), wc_s.at[0, 0], wc_r.at[0, 0])
         for step in range(2):
+            if step == 1:
+                take_x(2)
+                take_x(3)
             for d in range(2 * step, 2 * step + 2):
                 if d > 0:
                     arrive(slab(d, 1 - cc, plane, half), wc_s.at[0, d], wc_r.at[0, d])
@@ -251,15 +256,14 @@
             multiply(place)
             send(theirs.at[place], rbuf.at[place], ry_s.at[step], ry_r.at[step], ymate[1])
         for step in range(2):
-            place = flip(hh // 2, step)
-            arrive(rbuf.at[place], ry_s.at[step], ry_r.at[step])
-        for p in range(2):
+            p = flip(hh // 2, step)
+            arrive(rbuf.at[p], ry_s.at[step], ry_r.at[step])
             got = rbuf[p].astype(jnp.float32)
             low = jnp.where(uu == 0, mine[p], got)
             high = jnp.where(uu == 0, got, mine[p])
             cut = half_block // 2
             residual = jnp.concatenate([low[:, :cut], high[:, :cut], low[:, cut:], high[:, cut:]], axis=1)
-            place = slice(2 * p * half_block, 2 * (p + 1) * half_block)
+            place = pl.ds(pl.multiple_of(p * 2 * half_block, 2 * half_block), 2 * half_block)
             hidden[:, place] = (tokens_ref[:, place].astype(jnp.float32) + residual).astype(jnp.bfloat16)
     else:
         load_w.wait()
@@ -403,14 +407,16 @@
     for e in range(1, pairs):
         take_y(e, 0)
         take_y(e, 1)
+    take_z(2)
+    for e in range(1, pairs):
         take_c(e, 0)
         absorb_all(e, 0)
-    take_z(2)
     take_z(3)
+    for e in range(1, pairs):
+        take_y(e, 2)
     take_c(0, 1)
     absorb_all(0, 1)
     for e in range(1, pairs):
-        take_y(e, 2)
         take_y(e, 3)
     for e in range(1, pairs):
         take_c(e, 1)
@@ -433,19 +439,27 @@
             if t > 0:
                 send(osend.at[t], obuf.at[hh], o_s.at[t], o_r.at[t], zmate[t])
     obuf[hh] = osend[0]
+    load_out.wait()
+
+    def pair_product(owner):
+        weights = out_w[pl.ds(pl.multiple_of(owner * LANES, LANES), LANES), :]
+        return jnp.dot(obuf[owner, 0:rows, :], weights, preferred_element_type=jnp.float32)
+
+    projected_out = pair_product(hh)
     for d in range(1, SPLIT):
         arrive(obuf.at[flip(hh, d)], o_s.at[d], o_r.at[d])
-    load_out.wait()
-
-    parts = [obuf[g, 0:rows, :] for g in range(SPLIT)]
+        projected_out = projected_out + pair_product(flip(hh, d))
+    parts = []
     for g in range(0, SPLIT, 2):
         first = obuf[g, rows : rows + fold, :].astype(jnp.float32)
         second = obuf[g + 1, rows : rows + fold, :].astype(jnp.float32)
         upper = jnp.where(left[:fold], first, pltpu.roll(second, HEAD, 1))
         lower = jnp.where(left[:fold], pltpu.roll(first, HEAD, 1), second)
         parts.append(jnp.concatenate([upper, lower], axis=0).astype(jnp.bfloat16))
-    attended = jnp.concatenate(parts, axis=1)
-    projected_out = jnp.dot(attended, out_w[...], preferred_element_type=jnp.float32)
+    singles = jnp.concatenate(parts, axis=1)
+    projected_out = projected_out + jnp.dot(
+        singles, out_w[SPLIT * LANES :, :], preferred_element_type=jnp.float32
+    )
     result_ref[...] = (hidden[...].astype(jnp.float32) + mod_ref[2:3, :] * projected_out).astype(jnp.bfloat16)
 
     for copy in sent:

time: 64.8 us -> 62.4 us (0.963)
  Pallas kernels: 62.8 us -> 60.4 us
    pallas_call x1, Pallas kernels: 62.8 us -> 60.4 us  [per_device(): pl.pallas_call(functools.partial(kernel, n, gather), out_shape=jax.ShapeD...]
where the time goes in v4:
time: 62.4 us; the launch traced here: 62.2 us
  Pallas kernels  60.4 us (97%)
  local copies, waits for them, and re-layouts  1.77 us (3%)
    pallas_call x1, Pallas kernels, per_device(): pl.pallas_call(functools.partial(kernel, n, gather), out_shape=jax.ShapeD...  60.4 us
    unnamed x1, local copies, waits for them, and re-layouts  1.77 us

profile of v4, /device:TPU:0, one launch (start us, length us, event | category | flops | bytes accessed | tf_op | source)
XLA Modules:
  0.0 62.2 jit_solution(13240830856823315039)
XLA Ops:
  0.0 60.4 %shard_map.64 = bf16[128,1536]{1,0:T(8,128)(2,1)} custom-call(bf16[128,1536]{1,0:T(8,128)(2,1)} %tokens_hbm.1, bf16[128,1536]{1,0:T(8,128)(2,1)} %control_hbm.1, bf16[96,1536]{1,0:T(8,128)(2,1)} %bitcast.1, f32[3,1536]{1,0:T(4,128)} %mod_ref.1, bf16[1536,2304]{1,0:T(8,128)(2,1)} %qkv_hbm.1, bf16[768,1536]{1,0:T(8,128)(2,1)} %out_hbm.1), custom_call_target="tpu_custom_call" | custom-call | tf_op jit(solution)/shard_map/pallas_call | solution.py:483
  60.4 1.8 %copy.8 = bf16[128,1536]{1,0:T(8,128)(2,1)} copy(bf16[128,1536]{1,0:T(8,128)(2,1)} %shard_map.64) | data formatting | bytes 786432

commit v5 on v4

--- a/solution.py
+++ b/solution.py
@@ -11,7 +11,7 @@
 HEAD = 64
 GROUPS = 32
 VIEWS = 8
-EARLY_TILE = 512
+EARLY_TILE = 256
 LAST_TILE = 128
 SPLIT = 4
 LANES = 128
@@ -316,8 +316,14 @@
         single = jnp.concatenate([single, pltpu.roll(single, HEAD, 1)], axis=0)
         qbuf[d * rows : (d + 1) * rows, LANES : 2 * LANES] = jnp.where(left, single, 0.0).astype(jnp.bfloat16)
 
-    for d in range(1, SPLIT):
+    def send_q(d):
         send(qpack.at[flip(hh, d)], qpart(d), q_s.at[d], q_r.at[d], zmate[d])
+
+    def take_q(d):
+        arrive(qpart(d), q_s.at[d], q_r.at[d])
+        unfold_query(qin[d], d)
+
+    send_q(1)
     unfold_query(qpack[hh], 0)
 
     key = project(features)
@@ -391,37 +397,40 @@
             l_ref[h, mine_q, :] = total
             acc_ref[h, mine_q, :] = mixed
 
-    def absorb_all(e, part):
-        @pl.loop(0, SPLIT * rows // EARLY_TILE)
-        def _(t):
-            absorb(pl.multiple_of(t * EARLY_TILE, EARLY_TILE), EARLY_TILE, e, part)
+    near, far = 0, EARLY_TILE
 
     relay_kv(0)
-    for d in range(1, SPLIT):
-        arrive(qpart(d), q_s.at[d], q_r.at[d])
-        unfold_query(qin[d], d)
+    take_q(1)
     take_z(1)
     send_kv(SPLIT - 1)
+    send_q(2)
+    send_q(3)
     take_c(0, 0)
-    absorb_all(0, 0)
+    absorb(near, EARLY_TILE, 0, 0)
     for e in range(1, pairs):
         take_y(e, 0)
         take_y(e, 1)
     take_z(2)
     for e in range(1, pairs):
         take_c(e, 0)
-        absorb_all(e, 0)
+        absorb(near, EARLY_TILE, e, 0)
     take_z(3)
     for e in range(1, pairs):
         take_y(e, 2)
     take_c(0, 1)
-    absorb_all(0, 1)
+    absorb(near, EARLY_TILE, 0, 1)
     for e in range(1, pairs):
         take_y(e, 3)
+    take_q(2)
+    take_q(3)
+    for e in range(pairs):
+        absorb(far, EARLY_TILE, e, 0)
+    absorb(far, EARLY_TILE, 0, 1)
     for e in range(1, pairs):
         take_c(e, 1)
         if e < pairs - 1:
-            absorb_all(e, 1)
+            absorb(near, EARLY_TILE, e, 1)
+            absorb(far, EARLY_TILE, e, 1)
 
     deep = LAST_TILE
     for at_row in reversed(range(0, SPLIT * rows, deep)):

time: 62.4 us -> 63 us (level)
  no operation moved by 1% of the time
where the time goes in v5:
time: 63 us; the launch traced here: 62.8 us
  Pallas kernels  61 us (97%)
  local copies, waits for them, and re-layouts  1.77 us (3%)
    pallas_call x1, Pallas kernels, per_device(): pl.pallas_call(functools.partial(kernel, n, gather), out_shape=jax.ShapeD...  61 us
    unnamed x1, local copies, waits for them, and re-layouts  1.77 us

profile of v5, /device:TPU:0, one launch (start us, length us, event | category | flops | bytes accessed | tf_op | source)
XLA Modules:
  0.0 62.8 jit_solution(10933432307916122433)
XLA Ops:
  0.0 61.0 %shard_map.64 = bf16[128,1536]{1,0:T(8,128)(2,1)} custom-call(bf16[128,1536]{1,0:T(8,128)(2,1)} %tokens_hbm.1, bf16[128,1536]{1,0:T(8,128)(2,1)} %control_hbm.1, bf16[96,1536]{1,0:T(8,128)(2,1)} %bitcast.1, f32[3,1536]{1,0:T(4,128)} %mod_ref.1, bf16[1536,2304]{1,0:T(8,128)(2,1)} %qkv_hbm.1, bf16[768,1536]{1,0:T(8,128)(2,1)} %out_hbm.1), custom_call_target="tpu_custom_call" | custom-call | tf_op jit(solution)/shard_map/pallas_call | solution.py:492
  61.0 1.8 %copy.8 = bf16[128,1536]{1,0:T(8,128)(2,1)} copy(bf16[128,1536]{1,0:T(8,128)(2,1)} %shard_map.64) | data formatting | bytes 786432
